TPU v7x, 32 devices: a whole 2x2x4 slice. The times are simulated.
32 devices in a mesh: gx: 16 (over z, y, core), gy: 2 (over x).
Axes of the slice: x: 2, y: 2, z: 4, core: 2. Of those that a mesh axis runs over, the one named last changes fastest.
Arguments:
- adj_later: float32 [19, 128, 32, 256], P(None, 'gx', 'gy'), may hold values from -6 to 6
- saved_pops: bfloat16 [2, 19, 128, 32, 256], P(None, None, 'gx', 'gy'), may hold values from 0.015 to 0.49, as said below
- saved_scale: float32 [2, 19, 128, 32, 2], P(None, None, 'gx', 'gy'), may hold values from 0.7 to 1.4
- solid: int32 [128, 32, 256], P('gx', 'gy'), may hold values 0 or 1
- seed_values: float32 [4096, 19], P(('gx', 'gy')), may hold values from -12 to 12
- seed_contact: int32 [4096, 1], P(('gx', 'gy')), may hold values from 0 to 8; in each aligned block of 128 rows (0 to 127, 128 to 255, ...) at most 32 rows name the same one
- seed_cell: int32 [4096], P(('gx', 'gy')), may hold values from 0 to 32767
Outputs:
- adj_initial: float32 [19, 128, 32, 256], P(None, 'gx', 'gy')
- adj_middle: float32 [19, 128, 32, 256], P(None, 'gx', 'gy')
Inputs may be any that keep to these rules, and one draw needn't show every extreme that they name: `saved_pops`: each saved population is its lattice weight w_i times a factor between 0.55 and 1.45. `seed_contact`: among the items held by one device no contact code appears more than 32 times; some code reaches 32 on some device.
All inputs are finite; a program needn't handle non-finite values. No bound on the sum of `solid` on one device may be relied on, other than what follows from the above.
Results may differ from a plain program's by a relative error of at most 0.0003.
Values sent between devices are 32-bit elements; how exact they have to be, the bound alone decides.
A program may use at most 128 MiB of HBM per device.

v0:
```python
import functools

import jax
import jax.numpy as jnp
from jax import lax
from jax.experimental import pallas as pl
from jax.experimental.pallas import tpu as pltpu
from jax.sharding import PartitionSpec as P

LATTICE = [
    (0, 0, 0),
    (1, 0, 0),
    (-1, 0, 0),
    (0, 1, 0),
    (0, -1, 0),
    (0, 0, 1),
    (0, 0, -1),
    (1, 1, 0),
    (-1, -1, 0),
    (1, -1, 0),
    (-1, 1, 0),
    (1, 0, 1),
    (-1, 0, -1),
    (1, 0, -1),
    (-1, 0, 1),
    (0, 1, 1),
    (0, -1, -1),
    (0, 1, -1),
    (0, -1, 1),
]
OPPOSITE = [0, 2, 1, 4, 3, 6, 5, 8, 7, 10, 9, 12, 11, 14, 13, 16, 15, 18, 17]
CAP = 32
MESH = pl.DeviceIdType.MESH
F32 = jnp.float32

ORDER = [1, 7, 9, 11, 13, 2, 8, 10, 12, 14, 0, 3, 4, 5, 6, 15, 16, 17, 18]
SLOT = [ORDER.index(pop) for pop in range(19)]
Y_SETS = [[3, 7, 10, 15, 17], [4, 8, 9, 16, 18]]


def velocities(pops, scale, step, x, out):
    rows, height = pops.shape[3], pops.shape[4]
    blocks = scale.shape[2] // rows
    factors = [scale[step, x, pl.ds(b, rows, stride=blocks), :] for b in range(blocks)]
    f = []
    for pop in range(19):
        wide = jnp.concatenate(
            [jnp.broadcast_to(c[:, pop : pop + 1], (rows, height // blocks)) for c in factors], 1
        )
        f.append(pops[step, pop, x].astype(F32) * wide)
    plus = {k: f[k] + f[k + 1] for k in range(1, 19, 2)}
    minus = {k: f[k] - f[k + 1] for k in range(1, 19, 2)}
    density = f[0]
    for k in range(1, 19, 2):
        density = density + plus[k]
    inverse = 1.0 / density
    out[step, 0, x] = (minus[1] + minus[7] + minus[9] + minus[11] + minus[13]) * inverse
    out[step, 1, x] = (minus[3] + minus[7] - minus[9] + minus[15] + minus[17]) * inverse
    out[step, 2, x] = (minus[5] + minus[11] - minus[13] + minus[15] - minus[17]) * inverse


def adjoint_plane(field, slots, edge, velocity, solid, x, store):
    rows, height = field.shape[2], field.shape[3]
    row = lax.broadcasted_iota(jnp.int32, (rows, height), 0)
    col = lax.broadcasted_iota(jnp.int32, (rows, height), 1)
    h = []
    for pop in range(19):
        cx, cy, cz = LATTICE[pop]
        value = field[slots[pop], x + 1 + cx]
        if cy != 0:
            side = 0 if cy == 1 else 1
            place = Y_SETS[side].index(pop)
            line = edge[side, place, pl.ds(x + cx + 8, 1), :]
            turned = pltpu.roll(value, rows - 1 if cy == 1 else 1, 0)
            value = jnp.where(row == (rows - 1 if cy == 1 else 0), line, turned)
        if cz != 0:
            turned = pltpu.roll(value, height - 1 if cz == 1 else 1, 1)
            value = jnp.where(col == (height - 1 if cz == 1 else 0), 0.0, turned)
        h.append(value)
    s = {k: h[k] + h[k + 1] for k in range(1, 19, 2)}
    d = {k: h[k] - h[k + 1] for k in range(1, 19, 2)}
    diagonal = s[7] + s[9] + s[11] + s[13] + s[15] + s[17]
    total = 12.0 * h[0] + 2.0 * (s[1] + s[3] + s[5]) + diagonal
    ax = 2.0 * d[1] + d[7] + d[9] + d[11] + d[13]
    ay = 2.0 * d[3] + d[7] - d[9] + d[15] + d[17]
    az = 2.0 * d[5] + d[11] - d[13] + d[15] - d[17]
    bxx = 2.0 * s[1] + (s[7] + s[9]) + (s[11] + s[13])
    byy = 2.0 * s[3] + (s[7] + s[9]) + (s[15] + s[17])
    bzz = 2.0 * s[5] + (s[11] + s[13]) + (s[15] + s[17])
    bxy, bxz, byz = s[7] - s[9], s[11] - s[13], s[15] - s[17]
    ux, uy, uz = velocity[0, x], velocity[1, x], velocity[2, x]
    qx = bxx * ux + bxy * uy + bxz * uz
    qy = bxy * ux + byy * uy + byz * uz
    qz = bxz * ux + byz * uy + bzz * uz
    square = ux * ux + uy * uy + uz * uz
    factor = 1.25 / 36.0
    base = (factor * total) * (1.0 + 1.5 * square) - (4.5 * factor) * (ux * qx + uy * qy + uz * qz)
    pull = (3.0 * factor) * total
    mx = (3.0 * factor) * ax + (9.0 * factor) * qx - pull * ux
    my = (3.0 * factor) * ay + (9.0 * factor) * qy - pull * uy
    mz = (3.0 * factor) * az + (9.0 * factor) * qz - pull * uz
    along = {
        1: mx, 3: my, 5: mz, 7: mx + my, 9: mx - my,
        11: mx + mz, 13: mx - mz, 15: my + mz, 17: my - mz,
    }
    is_solid = solid[x] > 0
    store(0, jnp.where(is_solid, h[0], base - 0.25 * h[0]))
    for k in range(1, 19, 2):
        store(k, jnp.where(is_solid, h[k + 1], (base + along[k]) - 0.25 * h[k]))
        store(k + 1, jnp.where(is_solid, h[k], (base - along[k]) - 0.25 * h[k + 1]))


def kernel(
    n_gx, n_gy, adj, pops_in, scale_in, solid_in, values_in, contact_in, cell_in,
    out_mid, out_face, out_edge, out_velocity, later, middle, pops, scale, solid, velocity, seed_values, contact, cell,
    item_out, item_in, item_all, z_hot, face_out, edge_out, edge, nothing, in_sem, out_sem, nothing_sem, item_send, item_recv, face_send, face_recv,
):
    gx, gy = lax.axis_index("gx"), lax.axis_index("gy")
    wx, wy, height = adj.shape[1:]
    cells = wx * wy

    def here(ax, ay):
        px, py = gx + ax, gy + ay
        return (px >= 0) & (px < n_gx) & (py >= 0) & (py < n_gy)

    def at(ax, ay):
        return (gx + ax, gy + ay)

    around = [(ax, ay) for ax in (-1, 0, 1) for ay in (-1, 0, 1) if (ax, ay) != (0, 0)]

    copies = {}

    def fetch(name, index, source, target):
        copies[name] = pltpu.make_async_copy(source, target, in_sem.at[index])
        copies[name].start()

    fetch("contact", 5, contact_in, contact)
    fetch("cell", 6, cell_in, cell)
    fetch("values", 7, values_in, seed_values)
    fetch("pops1", 0, pops_in.at[1], pops.at[1])
    fetch("scale", 1, scale_in, scale)
    for slot in range(19):
        pltpu.make_async_copy(adj.at[ORDER[slot]], later.at[slot, pl.ds(1, wx)], in_sem.at[2]).start()
    fetch("solid", 3, solid_in, solid)
    fetch("pops0", 4, pops_in.at[0], pops.at[0])

    barrier = pltpu.get_barrier_semaphore()
    for ax, ay in around:
        @pl.when(here(ax, ay))
        def _(ax=ax, ay=ay):
            pl.semaphore_signal(barrier, inc=1, device_id=at(ax, ay), device_id_type=MESH)

    if n_gy == 2:
        other = 1 - 2 * gy
        routes = [(ax, rel) for ax in (-1, 0, 1) for rel in (0, 1)]
        shift_of = lambda rel: rel * other
    else:
        routes = [(ax, rel) for ax in (-1, 0, 1) for rel in (-1, 0, 1)]
        shift_of = lambda rel: rel
    back = {i: routes.index((-ax, rel if n_gy == 2 else -rel)) for i, (ax, rel) in enumerate(routes)}
    for name in ("contact", "cell", "values"):
        copies[name].wait()
    count = contact.shape[1]
    per_tile = 128 // CAP
    code = contact[...]
    code_across = jnp.broadcast_to(code, (count, count))
    first = lax.broadcasted_iota(jnp.int32, (count, count), 0)
    second = lax.broadcasted_iota(jnp.int32, (count, count), 1)
    same = (code_across == code_across.T) & (first < second)
    rank = jnp.sum(same.astype(jnp.int32), axis=0, keepdims=True)
    zeros = jnp.zeros((1, count), F32)
    values = [seed_values[pop : pop + 1, :] for pop in ORDER]
    top = jnp.concatenate(values + [zeros] * 5, 0)
    top_hi = top.astype(jnp.bfloat16)
    top_lo = (top - top_hi.astype(F32)).astype(jnp.bfloat16)
    place = cell[...]
    places = jnp.concatenate(
        [(place // height).astype(F32), (place % height).astype(F32)] + [zeros] * 14, 0
    ).astype(jnp.bfloat16)
    zero_rows = jnp.zeros((8, count), jnp.bfloat16)
    table = jnp.concatenate([top_hi, zero_rows, top_lo, zero_rows, places], 0)
    for i, (ax, rel) in enumerate(routes):
        lane = rank + CAP * (back[i] % per_tile)
        wanted = (ax + 1) * 3 + shift_of(rel) + 1
        lane = jnp.where(code == wanted, lane, -1)
        choose = (first == lane).astype(F32).astype(jnp.bfloat16)
        picked = lax.dot_general(
            table, choose, (((1,), (1,)), ((), ())), preferred_element_type=F32
        )
        tile = jnp.concatenate([picked[0:24] + picked[32:56], picked[64:72]], 0)
        if (ax, rel) == (0, 0):
            item_in[back[i]] = tile
        else:
            item_out[i] = tile

    def extent(position, size):
        return 1 + (position > 0).astype(jnp.int32) + (position < size - 1).astype(jnp.int32)

    pl.semaphore_wait(barrier, extent(gx, n_gx) * extent(gy, n_gy) - 1)

    def item_copy(i):
        ax, rel = routes[i]
        return pltpu.make_async_remote_copy(
            src_ref=item_out.at[i], dst_ref=item_in.at[back[i]],
            send_sem=item_send.at[i], recv_sem=item_recv.at[back[i]],
            device_id=at(ax, shift_of(rel)), device_id_type=MESH,
        )

    for i, (ax, rel) in enumerate(routes):
        if (ax, rel) != (0, 0):
            @pl.when(here(ax, shift_of(rel)))
            def _(i=i):
                item_copy(i).start()

            @pl.when(jnp.logical_not(here(ax, shift_of(rel))))
            def _(i=i):
                item_in[i] = jnp.zeros(item_in.shape[1:], F32)

    @pl.when(jnp.logical_not(here(1, 0)))
    def _():
        later[pl.ds(0, 5), wx + 1] = jnp.zeros((5, wy, height), F32)

    @pl.when(jnp.logical_not(here(-1, 0)))
    def _():
        later[pl.ds(5, 5), 0] = jnp.zeros((5, wy, height), F32)

    corners = []
    for side, ay in ((0, 1), (1, -1)):
        for pop in Y_SETS[side]:
            if LATTICE[pop][0] != 0:
                corners.append((side, Y_SETS[side].index(pop), LATTICE[pop][0], ay))
    for side, ay in ((0, 1), (1, -1)):
        @pl.when(jnp.logical_not(here(0, ay)))
        def _(side=side):
            edge[side, :, pl.ds(8, wx), :] = jnp.zeros((5, wx, height), F32)
    for side, slot, cx, ay in corners:
        @pl.when(jnp.logical_not(here(cx, ay)))
        def _(side=side, slot=slot, cx=cx):
            edge[side, slot, pl.ds(8 + 8 * cx, 8), :] = jnp.zeros((8, height), F32)

    nothing[...] = jnp.zeros(nothing.shape, F32)
    blanks = [(out_face.at[i], nothing, cx, 0) for i, cx in enumerate((1, -1))]
    for side, ay in ((0, 1), (1, -1)):
        blanks.append((out_edge.at[side, :, pl.ds(8, wx), :], nothing.at[:, pl.ds(0, wx)], 0, ay))
    for side, slot, cx, ay in corners:
        blanks.append(
            (out_edge.at[side, slot, pl.ds(8 + 8 * cx, 8), :], nothing.at[0, pl.ds(0, 8)], cx, ay)
        )

    def blank(i):
        target, source = blanks[i][:2]
        return pltpu.make_async_copy(source, target, nothing_sem.at[i])

    for i in range(len(blanks)):
        @pl.when(jnp.logical_not(here(*blanks[i][2:])))
        def _(i=i):
            blank(i).start()

    def x_copy(stage, cx):
        pops_slot = pl.ds(0 if cx == 1 else 5, 5)
        far = wx + 1 if cx == 1 else 0
        index = 0 if cx == 1 else 1
        return pltpu.make_async_remote_copy(
            src_ref=face_out.at[stage, index],
            dst_ref=later.at[pops_slot, far] if stage == 0 else out_face.at[index],
            send_sem=face_send.at[stage, index], recv_sem=face_recv.at[stage, index],
            device_id=at(-cx, 0), device_id_type=MESH,
        )

    def y_copy(stage, side):
        target = edge if stage == 0 else out_edge
        return pltpu.make_async_remote_copy(
            src_ref=edge_out.at[stage, side], dst_ref=target.at[side, :, pl.ds(8, wx), :],
            send_sem=face_send.at[stage, 2 + side], recv_sem=face_recv.at[stage, 2 + side],
            device_id=at(0, -1 if side == 0 else 1), device_id_type=MESH,
        )

    def corner_copy(stage, number):
        side, slot, cx, ay = corners[number]
        target = edge if stage == 0 else out_edge
        return pltpu.make_async_remote_copy(
            src_ref=edge_out.at[stage, side, slot],
            dst_ref=target.at[side, slot, pl.ds(8 + 8 * cx, 8), :],
            send_sem=face_send.at[stage, 4 + number], recv_sem=face_recv.at[stage, 4 + number],
            device_id=at(-cx, -ay), device_id_type=MESH,
        )

    x_links = [(lambda stage, cx=cx: x_copy(stage, cx), cx, 0) for cx in (1, -1)]
    y_links = [(lambda stage, side=side: y_copy(stage, side), 0, 1 if side == 0 else -1) for side in (0, 1)]
    y_links += [
        (lambda stage, number=number: corner_copy(stage, number), corners[number][2], corners[number][3])
        for number in range(4)
    ]

    def start(links, stage):
        for make, cx, cy in links:
            @pl.when(here(-cx, -cy))
            def _(make=make):
                make(stage).start()

    def arrive(links, stage):
        for make, cx, cy in links:
            @pl.when(here(cx, cy))
            def _(make=make):
                make(stage).wait_recv()

    copies["pops1"].wait()
    copies["scale"].wait()

    def late(x, carry):
        velocities(pops, scale, 1, x, velocity)
        return carry

    lax.fori_loop(0, wx, late, 0)
    pltpu.make_async_copy(adj, later.at[:, pl.ds(1, wx)], in_sem.at[2]).wait()
    for side in range(2):
        line = 0 if side == 0 else wy - 1
        for index, pop in enumerate(Y_SETS[side]):
            for x in range(wx):
                edge_out[0, side, index, x : x + 1, :] = later[SLOT[pop], 1 + x, line : line + 1, :]

    for i, (ax, rel) in enumerate(routes):
        if (ax, rel) != (0, 0):
            @pl.when(here(ax, shift_of(rel)))
            def _(i=i):
                pltpu.make_async_remote_copy(
                    src_ref=item_out.at[i], dst_ref=item_in.at[i],
                    send_sem=item_send.at[i], recv_sem=item_recv.at[i],
                    device_id=at(ax, shift_of(rel)), device_id_type=MESH,
                ).wait_recv()

    tiles = -(-len(routes) // per_tile)
    wide = tiles * 128
    gathered = []
    for t in range(tiles):
        part = item_in[t * per_tile]
        for i in range(t * per_tile + 1, min((t + 1) * per_tile, len(routes))):
            part = part + item_in[i]
        gathered.append(part)
    items = jnp.concatenate(gathered, 1)
    hi = items.astype(jnp.bfloat16).astype(F32)
    item_all[0] = hi
    item_all[1] = items - hi
    for t in range(tiles):
        z_row = jnp.broadcast_to(gathered[t][25:26, :], (128, 128))
        z_of = z_row.T.astype(jnp.int32)
        for b in range(height // 128):
            lanes = lax.broadcasted_iota(jnp.int32, (128, 128), 1) + 128 * b
            z_hot[pl.ds(128 * t, 128), pl.ds(128 * b, 128)] = (
                (z_of == lanes).astype(F32).astype(jnp.bfloat16)
            )
    xy_of = items[24:25, :].astype(jnp.int32)

    def at_cells(length, first, stride):
        number = lax.broadcasted_iota(jnp.int32, (length, wide), 0)
        return number * stride + first == jnp.broadcast_to(xy_of, (length, wide))

    def field_of(rows):
        spread = jnp.concatenate(
            [
                jnp.where(match, item_all[part, slot : slot + 1, :], 0.0)
                for part in range(2)
                for slot, match in rows
            ],
            0,
        ).astype(jnp.bfloat16)
        both = jnp.dot(spread, z_hot[...], preferred_element_type=F32)
        half = both.shape[0] // 2
        return both[:half] + both[half:]

    near = [at_cells(wy, 0, 1), at_cells(wy, (wx - 1) * wy, 1)]
    line_of = [at_cells(wx, 0, wy), at_cells(wx, wy - 1, wy)]
    rows = [(5 * i + j, near[i]) for i in range(2) for j in range(5)]
    rows += [(SLOT[pop], line_of[side]) for side in range(2) for pop in Y_SETS[side]]
    outer = field_of(rows)
    for i in range(2):
        plane = later[pl.ds(5 * i, 5), 1 if i == 0 else wx]
        face_out[0, i] = plane + outer[5 * wy * i : 5 * wy * (i + 1)].reshape(5, wy, height)
    start(x_links, 0)
    begin = 10 * wy
    for side in range(2):
        part = outer[begin + 5 * wx * side : begin + 5 * wx * (side + 1)]
        edge_out[0, side] = edge_out[0, side] + part.reshape(5, wx, height)
    start(y_links, 0)

    def add_seeds(x, carry):
        match = at_cells(wy, x * wy, 1)
        seeds = field_of([(slot, match) for slot in range(19)])
        later[:, x + 1] = later[:, x + 1] + seeds.reshape(19, wy, height)
        return carry

    lax.fori_loop(0, wx, add_seeds, 0)
    copies["solid"].wait()

    def write(x):
        return pltpu.make_async_copy(middle.at[:, x], out_mid.at[:, x], out_sem.at[1 + x])

    def middle_plane(x, face=None):
        def store(pop, value):
            middle[pop, x] = value
            cx, cy = LATTICE[pop][:2]
            if cy != 0:
                side, line = (0, 0) if cy == 1 else (1, wy - 1)
                edge_out[1, side, Y_SETS[side].index(pop), pl.ds(x, 1), :] = value[line : line + 1, :]
            if face is not None and SLOT[pop] // 5 == face:
                face_out[1, face, SLOT[pop] % 5] = value

        adjoint_plane(later, SLOT, edge, velocity.at[1], solid, x, store)
        write(x).start()

    arrive(y_links, 0)
    arrive(x_links, 0)
    middle_plane(0, 0)
    middle_plane(wx - 1, 1)
    start(x_links, 1)

    def inner(x, carry):
        middle_plane(x)
        return carry

    lax.fori_loop(1, wx - 1, inner, 0)
    start(y_links, 1)

    copies["pops0"].wait()

    def early(x, carry):
        velocities(pops, scale, 0, x, velocity)
        return carry

    lax.fori_loop(0, wx, early, 0)
    velocity_write = pltpu.make_async_copy(velocity.at[0], out_velocity, out_sem.at[0])
    velocity_write.start()

    for i, (ax, rel) in enumerate(routes):
        if (ax, rel) != (0, 0):
            @pl.when(here(ax, shift_of(rel)))
            def _(i=i):
                item_copy(i).wait_send()
    for stage in range(2):
        for make, cx, cy in x_links + y_links:
            @pl.when(here(-cx, -cy))
            def _(make=make, stage=stage):
                make(stage).wait_send()
    for i in range(len(blanks)):
        @pl.when(jnp.logical_not(here(*blanks[i][2:])))
        def _(i=i):
            blank(i).wait()
    for x in range(wx):
        write(x).wait()
    velocity_write.wait()
    arrive(y_links, 1)
    arrive(x_links, 1)


def last_kernel(
    mid, face, edge_in, velocity_in, solid_in, out_init, out_mid,
    field, initial, edge, velocity, solid, side_sem, plane_sem, out_sem,
):
    wx = mid.shape[1]
    small = [
        pltpu.make_async_copy(velocity_in, velocity, side_sem.at[0]),
        pltpu.make_async_copy(solid_in, solid, side_sem.at[1]),
    ]
    for side in range(2):
        for index, pop in enumerate(Y_SETS[side]):
            cx = LATTICE[pop][0]
            span = pl.ds(0 if cx == -1 else 8, 8 if cx == 0 else 16)
            small.append(
                pltpu.make_async_copy(
                    edge_in.at[side, index, span, :], edge.at[side, index, span, :],
                    side_sem.at[2 + 5 * side + index],
                )
            )

    def face_copy(i, j):
        pop = ORDER[5 * i + j]
        return pltpu.make_async_copy(
            face.at[i, j], field.at[pop, wx + 1 if i == 0 else 0], plane_sem.at[wx + 5 * i + j]
        )

    def plane_copy(x):
        return pltpu.make_async_copy(mid.at[:, x], field.at[:, x + 1], plane_sem.at[x])

    def plane_write(x):
        return pltpu.make_async_copy(field.at[:, x + 1], out_mid.at[:, x], out_sem.at[x])

    def write(x):
        return pltpu.make_async_copy(initial.at[:, x], out_init.at[:, x], out_sem.at[wx + x])

    for j in range(5):
        face_copy(1, j).start()
    plane_copy(0).start()
    for copy in small:
        copy.start()
    for x in range(1, wx):
        plane_copy(x).start()
    for j in range(5):
        face_copy(0, j).start()

    def plane(x):
        def store(pop, value):
            initial[pop, x] = value

        adjoint_plane(field, list(range(19)), edge, velocity, solid, x, store)
        write(x).start()

    for j in range(5):
        face_copy(1, j).wait()
    plane_copy(0).wait()
    plane_write(0).start()
    for copy in small:
        copy.wait()

    def inner(x, carry):
        plane_copy(x + 1).wait()
        plane_write(x + 1).start()
        plane(x)
        return carry

    lax.fori_loop(0, wx - 1, inner, 0)
    for j in range(5):
        face_copy(0, j).wait()
    plane(wx - 1)
    for x in range(wx):
        plane_write(x).wait()
        write(x).wait()


def body(n_gx, n_gy, adj_later, saved_pops, saved_scale, solid, seed_values, seed_contact, seed_cell):
    channels, wx, wy, height = adj_later.shape
    blocks = saved_scale.shape[-1]
    count = seed_cell.shape[0]
    scale = saved_scale.transpose(0, 2, 3, 4, 1).reshape(2, wx, wy * blocks, channels)
    routes = 6 if n_gy == 2 else 9
    wide = -(-routes * CAP // 128) * 128
    field = (channels, wx, wy, height)
    in_hbm = pl.BlockSpec(memory_space=pltpu.HBM)
    shape = lambda *dims: jax.ShapeDtypeStruct(dims, F32)
    params = dict(has_side_effects=True, vmem_limit_bytes=60 * 1024 * 1024)
    mid, face, edge, velocity = pl.pallas_call(
        functools.partial(kernel, n_gx, n_gy),
        out_shape=[
            shape(*field), shape(2, 5, wy, height), shape(2, 5, wx + 16, height),
            shape(3, wx, wy, height),
        ],
        in_specs=[in_hbm] * 7,
        out_specs=[in_hbm] * 4,
        scratch_shapes=[
            pltpu.VMEM((channels, wx + 2, wy, height), F32),
            pltpu.VMEM(field, F32),
            pltpu.VMEM((2,) + field, jnp.bfloat16),
            pltpu.VMEM(scale.shape, F32),
            pltpu.VMEM((wx, wy, height), jnp.int32),
            pltpu.VMEM((2, 3, wx, wy, height), F32),
            pltpu.VMEM((channels, count), F32),
            pltpu.VMEM((1, count), jnp.int32),
            pltpu.VMEM((1, count), jnp.int32),
            pltpu.VMEM((routes, 32, 128), F32),
            pltpu.VMEM((routes, 32, 128), F32),
            pltpu.VMEM((2, 32, wide), F32),
            pltpu.VMEM((wide, height), jnp.bfloat16),
            pltpu.VMEM((2, 2, 5, wy, height), F32),
            pltpu.VMEM((2, 2, 5, wx, height), F32),
            pltpu.VMEM((2, 5, wx + 16, height), F32),
            pltpu.VMEM((5, wy, height), F32),
            pltpu.SemaphoreType.DMA((8,)),
            pltpu.SemaphoreType.DMA((1 + wx,)),
            pltpu.SemaphoreType.DMA((8,)),
            pltpu.SemaphoreType.DMA((routes,)),
            pltpu.SemaphoreType.DMA((routes,)),
            pltpu.SemaphoreType.DMA((2, 8)),
            pltpu.SemaphoreType.DMA((2, 8)),
        ],
        compiler_params=pltpu.CompilerParams(collective_id=0, **params),
    )(
        adj_later, saved_pops, scale, solid, seed_values.T,
        seed_contact.reshape(1, count), seed_cell.reshape(1, count),
    )
    return pl.pallas_call(
        last_kernel,
        out_shape=[shape(*field)] * 2,
        in_specs=[in_hbm] * 5,
        out_specs=[in_hbm] * 2,
        scratch_shapes=[
            pltpu.VMEM((channels, wx + 2, wy, height), F32),
            pltpu.VMEM(field, F32),
            pltpu.VMEM((2, 5, wx + 16, height), F32),
            pltpu.VMEM((3, wx, wy, height), F32),
            pltpu.VMEM((wx, wy, height), jnp.int32),
            pltpu.SemaphoreType.DMA((12,)),
            pltpu.SemaphoreType.DMA((wx + 10,)),
            pltpu.SemaphoreType.DMA((2 * wx,)),
        ],
        compiler_params=pltpu.CompilerParams(vmem_limit_bytes=60 * 1024 * 1024),
    )(mid, face, edge, velocity, solid)


def solution(mesh):
    n_gx, n_gy = mesh.shape["gx"], mesh.shape["gy"]
    return jax.shard_map(
        functools.partial(body, n_gx, n_gy),
        mesh=mesh,
        in_specs=(
            P(None, "gx", "gy", None),
            P(None, None, "gx", "gy", None),
            P(None, None, "gx", "gy", None),
            P("gx", "gy", None),
            P(("gx", "gy"), None),
            P(("gx", "gy"), None),
            P(("gx", "gy")),
        ),
        out_specs=(P(None, "gx", "gy", None), P(None, "gx", "gy", None)),
        check_vma=False,
    )
```

profile of v0, /device:TPU:0, one launch (start us, length us, event | category | flops | bytes accessed | tf_op | source)
XLA Modules:
  0.0 20.8 jit_solution(9684584461124839041)
XLA Ops:
  0.6 15.7 %shard_map.86 = (f32[19,8,16,256]{3,2,1,0:T(8,128)}, f32[2,5,16,256]{3,2,1,0:T(8,128)}, f32[2,5,24,256]{3,2,1,0:T(8,128)}, f32[3,8,16,256]{3,2,1,0:T(8,128)}) custom-call(f32[19,8,16,256]{3,2,1,0:T(8,128)} %adj.1, bf16[2,19,8,16,256]{4,3,2,1,0:T(8,128)(2,1)} %pops_in.1, f32[2,8,32,19]{3,2,1,0:T(8,128)} %bitcast.6, s32[8,16,256]{2,1,0:T(8,128)} %solid_in.3, ...), custom_call_target="tpu_custom_call" | custom-call | tf_op jit(solution)/shard_map/pallas_call | solution.py:540
  16.4 4.4 %shard_map.87 = (f32[19,8,16,256]{3,2,1,0:T(8,128)}, f32[19,8,16,256]{3,2,1,0:T(8,128)}) custom-call(f32[19,8,16,256]{3,2,1,0:T(8,128)} %get-tuple-element.6.mid, f32[2,5,16,256]{3,2,1,0:T(8,128)} %get-tuple-element.7.face, f32[2,5,24,256]{3,2,1,0:T(8,128)} %get-tuple-element.8.edge_in, f32[3,8,16,256]{3,2,1,0:T(8,128)} %get-tuple-element.9.velocity_in, ...), custom_call_target="tpu_custom_call" | custom-call | tf_op jit(solution)/shard_map/pallas_call | solution.py:579
where the time goes:
time: 21 us; the launch traced here: 20.8 us
  Pallas kernels  20.1 us (96%)
  between operations  0.64 us (3%)
    pallas_call x1, Pallas kernels, body(): pl.pallas_call(functools.partial(kernel, n_gx, n_gy), out_shape=[shape(*f...  15.7 us
    pallas_call x1, Pallas kernels, body(): pl.pallas_call(last_kernel, out_shape=[shape(*field)] * 2, in_specs=[in_h...  4.4 us

commit v1 on v0

--- a/solution.py
+++ b/solution.py
@@ -41,42 +41,74 @@
 def velocities(pops, scale, step, x, out):
     rows, height = pops.shape[3], pops.shape[4]
     blocks = scale.shape[2] // rows
-    factors = [scale[step, x, pl.ds(b, rows, stride=blocks), :] for b in range(blocks)]
-    f = []
-    for pop in range(19):
-        wide = jnp.concatenate(
-            [jnp.broadcast_to(c[:, pop : pop + 1], (rows, height // blocks)) for c in factors], 1
-        )
-        f.append(pops[step, pop, x].astype(F32) * wide)
-    plus = {k: f[k] + f[k + 1] for k in range(1, 19, 2)}
-    minus = {k: f[k] - f[k + 1] for k in range(1, 19, 2)}
-    density = f[0]
-    for k in range(1, 19, 2):
-        density = density + plus[k]
-    inverse = 1.0 / density
-    out[step, 0, x] = (minus[1] + minus[7] + minus[9] + minus[11] + minus[13]) * inverse
-    out[step, 1, x] = (minus[3] + minus[7] - minus[9] + minus[15] + minus[17]) * inverse
-    out[step, 2, x] = (minus[5] + minus[11] - minus[13] + minus[15] - minus[17]) * inverse
+    length = height // blocks
+    for b in range(blocks):
+        span = pl.ds(b * length, length)
+        factors = scale[step, x, pl.ds(b, rows, stride=blocks), :]
+
+        def population(pop):
+            stored = pops[step, pop, x, :, span].astype(F32)
+            return stored * jnp.broadcast_to(factors[:, pop : pop + 1], (rows, length))
+
+        density = population(0)
+        momentum = [None, None, None]
+        for k in range(1, 19, 2):
+            plus, minus = population(k), population(k + 1)
+            density = density + (plus + minus)
+            change = plus - minus
+            for axis in range(3):
+                sign = LATTICE[k][axis]
+                if momentum[axis] is None and sign == 1:
+                    momentum[axis] = change
+                elif sign == 1:
+                    momentum[axis] = momentum[axis] + change
+                elif sign == -1:
+                    momentum[axis] = momentum[axis] - change
+        inverse = 1.0 / density
+        for axis in range(3):
+            out[step, axis, x, :, span] = momentum[axis] * inverse
 
 
 def adjoint_plane(field, slots, edge, velocity, solid, x, store):
     rows, height = field.shape[2], field.shape[3]
-    row = lax.broadcasted_iota(jnp.int32, (rows, height), 0)
-    col = lax.broadcasted_iota(jnp.int32, (rows, height), 1)
-    h = []
-    for pop in range(19):
-        cx, cy, cz = LATTICE[pop]
-        value = field[slots[pop], x + 1 + cx]
-        if cy != 0:
+    for r in range(rows // 8):
+        for c in range(height // 128):
+            adjoint_tile(field, slots, edge, velocity, solid, x, r, c, store)
+
+
+def adjoint_tile(field, slots, edge, velocity, solid, x, r, c, store):
+    rows, height = field.shape[2], field.shape[3]
+    row = lax.broadcasted_iota(jnp.int32, (8, 128), 0)
+    col = lax.broadcasted_iota(jnp.int32, (8, 128), 1)
+
+    def along_y(pop, c):
+        cx, cy = LATTICE[pop][:2]
+        span = pl.ds(c * 128, 128)
+        value = field[slots[pop], x + 1 + cx, pl.ds(r * 8, 8), span]
+        if cy == 0:
+            return value
+        beyond = r * 8 + (8 if cy == 1 else -1)
+        if 0 <= beyond < rows:
+            line = field[slots[pop], x + 1 + cx, pl.ds(beyond, 1), span]
+        else:
             side = 0 if cy == 1 else 1
-            place = Y_SETS[side].index(pop)
-            line = edge[side, place, pl.ds(x + cx + 8, 1), :]
-            turned = pltpu.roll(value, rows - 1 if cy == 1 else 1, 0)
-            value = jnp.where(row == (rows - 1 if cy == 1 else 0), line, turned)
-        if cz != 0:
-            turned = pltpu.roll(value, height - 1 if cz == 1 else 1, 1)
-            value = jnp.where(col == (height - 1 if cz == 1 else 0), 0.0, turned)
-        h.append(value)
+            line = edge[side, Y_SETS[side].index(pop), pl.ds(x + cx + 8, 1), :]
+            line = line[:, c * 128 : (c + 1) * 128]
+        turned = pltpu.roll(value, 7 if cy == 1 else 1, 0)
+        return jnp.where(row == (7 if cy == 1 else 0), jnp.broadcast_to(line, (8, 128)), turned)
+
+    def moved(pop):
+        cz = LATTICE[pop][2]
+        value = along_y(pop, c)
+        if cz == 0:
+            return value
+        shift = 127 if cz == 1 else 1
+        beyond = 0.0
+        if 0 <= c + cz < height // 128:
+            beyond = pltpu.roll(along_y(pop, c + cz), shift, 1)
+        return jnp.where(col == (127 if cz == 1 else 0), beyond, pltpu.roll(value, shift, 1))
+
+    h = [moved(pop) for pop in range(19)]
     s = {k: h[k] + h[k + 1] for k in range(1, 19, 2)}
     d = {k: h[k] - h[k + 1] for k in range(1, 19, 2)}
     diagonal = s[7] + s[9] + s[11] + s[13] + s[15] + s[17]
@@ -88,7 +120,8 @@
     byy = 2.0 * s[3] + (s[7] + s[9]) + (s[15] + s[17])
     bzz = 2.0 * s[5] + (s[11] + s[13]) + (s[15] + s[17])
     bxy, bxz, byz = s[7] - s[9], s[11] - s[13], s[15] - s[17]
-    ux, uy, uz = velocity[0, x], velocity[1, x], velocity[2, x]
+    here = (pl.ds(r * 8, 8), pl.ds(c * 128, 128))
+    ux, uy, uz = [velocity[(axis, x) + here] for axis in range(3)]
     qx = bxx * ux + bxy * uy + bxz * uz
     qy = bxy * ux + byy * uy + byz * uz
     qz = bxz * ux + byz * uy + bzz * uz
@@ -103,11 +136,11 @@
         1: mx, 3: my, 5: mz, 7: mx + my, 9: mx - my,
         11: mx + mz, 13: mx - mz, 15: my + mz, 17: my - mz,
     }
-    is_solid = solid[x] > 0
-    store(0, jnp.where(is_solid, h[0], base - 0.25 * h[0]))
+    is_solid = solid[(x,) + here] > 0
+    store(0, r, c, jnp.where(is_solid, h[0], base - 0.25 * h[0]))
     for k in range(1, 19, 2):
-        store(k, jnp.where(is_solid, h[k + 1], (base + along[k]) - 0.25 * h[k]))
-        store(k + 1, jnp.where(is_solid, h[k], (base - along[k]) - 0.25 * h[k + 1]))
+        store(k, r, c, jnp.where(is_solid, h[k + 1], (base + along[k]) - 0.25 * h[k]))
+        store(k + 1, r, c, jnp.where(is_solid, h[k], (base - along[k]) - 0.25 * h[k + 1]))
 
 
 def kernel(
@@ -396,14 +429,20 @@
         return pltpu.make_async_copy(middle.at[:, x], out_mid.at[:, x], out_sem.at[1 + x])
 
     def middle_plane(x, face=None):
-        def store(pop, value):
-            middle[pop, x] = value
+        lines = {}
+
+        def store(pop, r, c, value):
+            span = pl.ds(c * 128, 128)
+            middle[pop, x, pl.ds(r * 8, 8), span] = value
             cx, cy = LATTICE[pop][:2]
-            if cy != 0:
-                side, line = (0, 0) if cy == 1 else (1, wy - 1)
-                edge_out[1, side, Y_SETS[side].index(pop), pl.ds(x, 1), :] = value[line : line + 1, :]
+            if (cy == 1 and r == 0) or (cy == -1 and r == wy // 8 - 1):
+                side, line = (0, 0) if cy == 1 else (1, 7)
+                lines.setdefault(pop, []).append(value[line : line + 1])
+                if c == height // 128 - 1:
+                    whole = jnp.concatenate(lines[pop], 1)
+                    edge_out[1, side, Y_SETS[side].index(pop), pl.ds(x, 1), :] = whole
             if face is not None and SLOT[pop] // 5 == face:
-                face_out[1, face, SLOT[pop] % 5] = value
+                face_out[1, face, SLOT[pop] % 5, pl.ds(r * 8, 8), span] = value
 
         adjoint_plane(later, SLOT, edge, velocity.at[1], solid, x, store)
         write(x).start()
@@ -498,8 +537,8 @@
         face_copy(0, j).start()
 
     def plane(x):
-        def store(pop, value):
-            initial[pop, x] = value
+        def store(pop, r, c, value):
+            initial[pop, x, pl.ds(r * 8, 8), pl.ds(c * 128, 128)] = value
 
         adjoint_plane(field, list(range(19)), edge, velocity, solid, x, store)
         write(x).start()

time: 21 us -> 21.2 us (level)
  no operation moved by 1% of the time
where the time goes in v1:
time: 21.2 us; the launch traced here: 20.9 us
  Pallas kernels  20.3 us (96%)
  between operations  0.64 us (3%)
    pallas_call x1, Pallas kernels, body(): pl.pallas_call(functools.partial(kernel, n_gx, n_gy), out_shape=[shape(*f...  15.9 us
    pallas_call x1, Pallas kernels, body(): pl.pallas_call(last_kernel, out_shape=[shape(*field)] * 2, in_specs=[in_h...  4.41 us

profile of v1, /device:TPU:0, one launch (start us, length us, event | category | flops | bytes accessed | tf_op | source)
XLA Modules:
  0.0 20.9 jit_solution(5880314949976142264)
XLA Ops:
  0.6 15.9 %shard_map.86 = (f32[19,8,16,256]{3,2,1,0:T(8,128)}, f32[2,5,16,256]{3,2,1,0:T(8,128)}, f32[2,5,24,256]{3,2,1,0:T(8,128)}, f32[3,8,16,256]{3,2,1,0:T(8,128)}) custom-call(f32[19,8,16,256]{3,2,1,0:T(8,128)} %adj.1, bf16[2,19,8,16,256]{4,3,2,1,0:T(8,128)(2,1)} %pops_in.1, f32[2,8,32,19]{3,2,1,0:T(8,128)} %bitcast.6, s32[8,16,256]{2,1,0:T(8,128)} %solid_in.3, ...), custom_call_target="tpu_custom_call" | custom-call | tf_op jit(solution)/shard_map/pallas_call | solution.py:579
  16.5 4.4 %shard_map.87 = (f32[19,8,16,256]{3,2,1,0:T(8,128)}, f32[19,8,16,256]{3,2,1,0:T(8,128)}) custom-call(f32[19,8,16,256]{3,2,1,0:T(8,128)} %get-tuple-element.6.mid, f32[2,5,16,256]{3,2,1,0:T(8,128)} %get-tuple-element.7.face, f32[2,5,24,256]{3,2,1,0:T(8,128)} %get-tuple-element.8.edge_in, f32[3,8,16,256]{3,2,1,0:T(8,128)} %get-tuple-element.9.velocity_in, ...), custom_call_target="tpu_custom_call" | custom-call | tf_op jit(solution)/shard_map/pallas_call | solution.py:618
